TPU v7x, 128 devices: a whole 4x4x4 slice. The times are simulated.
128 devices in a mesh: dp: 4 (over y_lo, core), seq: 32 (over x, y_hi, z).
Axes of the slice: x: 4, y: 4 (y_hi: 2, y_lo: 2; y = y_hi * 2 + y_lo), z: 4, core: 2. Of those that a mesh axis runs over, the one named last changes fastest.
Arguments:
- siblings: int32 [4, 64, 16], P('dp', 'seq'), may hold values from 0 to 63, all different within a row
- queries: bfloat16 [4, 64, 512, 2560], P('dp', 'seq'), may hold values from -6 to 6
- grad_out: bfloat16 [4, 64, 512, 2560], P('dp', 'seq'), may hold values from -6 to 6
- keys_in: bfloat16 [4, 64, 16, 512], P('dp', 'seq'), may hold values from -4 to 4
- input_values: bfloat16 [4, 64, 16, 512], P('dp', 'seq'), may hold values from -6 to 6
- summary: bfloat16 [4, 64, 16, 5120], P('dp', 'seq'), may hold values from -6 to 6
Outputs:
- query_gradient: bfloat16 [4, 64, 512, 2560], P('dp', 'seq')
- kv_weight_grad: float32 [5120, 1024], P(('dp', 'seq'))
Inputs may be any that keep to these rules, and one draw needn't show every extreme that they name: `siblings`: the 16 entries of one completion's list are distinct completions of the same prompt.
All inputs are finite; a program needn't handle non-finite values.
Results may differ from a plain program's by a relative error of at most 0.012.
Values may be sent and summed in bfloat16 or wider, within the bound.
A program may use at most 192 MiB of HBM per device.

v0:
```python
import math
import jax
import jax.numpy as jnp
from jax import lax
from jax.sharding import PartitionSpec as P

HEAD_SIZE = 128


def group_grads(query_tile_block, incoming_gradient, key_tile_block, value_tile_block, scaling):
    scores = (
        jnp.einsum(
            "ctrd,cld->crtl", query_tile_block, key_tile_block, preferred_element_type=jnp.float32
        )
        * scaling
    )
    largest = jnp.max(scores, axis=-1, keepdims=True)
    exponent = jnp.exp(scores - largest)
    probability = exponent / jnp.sum(exponent, axis=-1, keepdims=True)
    prob_half = probability.astype(jnp.bfloat16)
    attended = jnp.einsum(
        "crtl,cld->ctrd", prob_half, value_tile_block, preferred_element_type=jnp.float32
    )
    token_delta = jnp.sum(incoming_gradient * attended, axis=-1)
    row_delta = jnp.transpose(token_delta, (0, 2, 1))[..., None]
    prob_grad = jnp.einsum(
        "ctrd,cld->crtl", incoming_gradient, value_tile_block, preferred_element_type=jnp.float32
    )
    score_half = (probability * (prob_grad - row_delta)).astype(jnp.bfloat16)
    query_gradient = (
        jnp.einsum("crtl,cld->ctrd", score_half, key_tile_block, preferred_element_type=jnp.float32)
        * scaling
    )
    key_gradient = (
        jnp.einsum(
            "crtl,ctrd->cld", score_half, query_tile_block, preferred_element_type=jnp.float32
        )
        * scaling
    )
    value_gradient = jnp.einsum(
        "crtl,ctrd->cld", prob_half, incoming_gradient, preferred_element_type=jnp.float32
    )
    return (query_gradient, key_gradient, value_gradient)


def per_device(siblings, queries, grad_out, keys_in, input_values, summary):
    keys_all, values_all = (
        lax.all_gather(keys_in, "seq", axis=1, tiled=True),
        lax.all_gather(input_values, "seq", axis=1, tiled=True),
    )
    sibling = siblings[0]
    own_count, row_length = (queries.shape[1], queries.shape[2])
    everyone = keys_all.shape[1]
    neighbours, positions, key_value_width = (sibling.shape[1], keys_in.shape[2], keys_in.shape[3])
    kv_heads = key_value_width // HEAD_SIZE
    group_span = queries.shape[3] // kv_heads
    group_size = group_span // HEAD_SIZE
    scaling = 1.0 / math.sqrt(HEAD_SIZE)
    key_rows = keys_all[0][sibling].reshape(own_count, neighbours * positions, key_value_width)
    value_rows = values_all[0][sibling].reshape(own_count, neighbours * positions, key_value_width)
    query_parts, key_parts, value_parts = ([], [], [])
    for kv_head in range(kv_heads):
        query_tile_block = queries[
            0, :, :, kv_head * group_span : (kv_head + 1) * group_span
        ].reshape(own_count, row_length, group_size, HEAD_SIZE)
        incoming_gradient = grad_out[
            0, :, :, kv_head * group_span : (kv_head + 1) * group_span
        ].reshape(own_count, row_length, group_size, HEAD_SIZE)
        key_tile_block = key_rows[:, :, kv_head * HEAD_SIZE : (kv_head + 1) * HEAD_SIZE]
        value_tile_block = value_rows[:, :, kv_head * HEAD_SIZE : (kv_head + 1) * HEAD_SIZE]
        query_gradient, key_gradient, value_gradient = group_grads(
            query_tile_block, incoming_gradient, key_tile_block, value_tile_block, scaling
        )
        query_parts.append(query_gradient.reshape(own_count, row_length, group_span))
        key_parts.append(key_gradient)
        value_parts.append(value_gradient)
    query_out = jnp.concatenate(query_parts, axis=-1).astype(jnp.bfloat16)
    key_gradient = jnp.concatenate(key_parts, axis=-1).reshape(
        own_count * neighbours, positions * key_value_width
    )
    value_gradient = jnp.concatenate(value_parts, axis=-1).reshape(
        own_count * neighbours, positions * key_value_width
    )
    targets = sibling.reshape(-1)
    placing = (targets[:, None] == jnp.arange(everyone, dtype=jnp.int32)[None, :]).astype(
        jnp.float32
    )
    key_buffer = jnp.dot(placing.T, key_gradient, precision=lax.Precision.HIGHEST)
    value_buffer = jnp.dot(placing.T, value_gradient, precision=lax.Precision.HIGHEST)
    owner_keys, owner_values = (
        lax.psum_scatter(key_buffer, "seq", scatter_dimension=0, tiled=True),
        lax.psum_scatter(value_buffer, "seq", scatter_dimension=0, tiled=True),
    )
    grads_half = jnp.concatenate(
        [
            owner_keys.astype(jnp.bfloat16).reshape(own_count * positions, key_value_width),
            owner_values.astype(jnp.bfloat16).reshape(own_count * positions, key_value_width),
        ],
        axis=1,
    )
    hidden = summary[0].reshape(own_count * positions, summary.shape[3])
    weight_grad = lax.psum_scatter(
        jnp.einsum("sd,sk->dk", hidden, grads_half, preferred_element_type=jnp.float32),
        ("dp", "seq"),
        scatter_dimension=0,
        tiled=True,
    )
    return (query_out[None], weight_grad)


def solution(mesh):
    placed = (
        P("dp", "seq", None),
        P("dp", "seq", None, None),
        P("dp", "seq", None, None),
        P("dp", "seq", None, None),
        P("dp", "seq", None, None),
        P("dp", "seq", None, None),
    )
    return jax.shard_map(
        per_device,
        mesh=mesh,
        in_specs=placed,
        out_specs=(P("dp", "seq", None, None), P(("dp", "seq"), None)),
        check_vma=False,
    )
```

profile of v0, /device:TPU:1, one launch (start us, length us, event | category | flops | bytes accessed | tf_op | source)
XLA Modules:
  0.0 1172.4 jit_solution(1729174952819636855)
XLA Ops:
  10.2 4.6 fusion.72
  14.8 2.4 copy.211
  17.2 2.5 copy.215
  19.7 1.5 copy.213
  21.2 1.5 copy.217
  22.7 4.6 fusion.73
  27.9 1.6 copy.216
  29.5 2.4 copy.214
  32.0 2.4 copy.218
  35.6 43.3 %all-gather.5.cloned.1.call-done = bf16[1,64,16,512]{3,2,0,1:T(8,128)(2,1)} async-done(((bf16[1,2,16,512]{3,2,0,1:T(8,128)(2,1)}), bf16[1,64,16,512]{3,2,0,1:T(8,128)(2,1)}) %all-gather.5.cloned.1.call-update) | async-done | bytes 1048592 | tf_op jit(solution)/shard_map/all_gather | solution.py:49
  79.0 2.6 gather_fusion.1
  81.6 63.8 %all-gather.3.cloned.1.call-done = bf16[1,64,16,512]{3,2,0,1:T(8,128)(2,1)} async-done(((bf16[1,2,16,512]{3,2,0,1:T(8,128)(2,1)}), bf16[1,64,16,512]{3,2,0,1:T(8,128)(2,1)}) %all-gather.3.cloned.1.call-update) | async-done | bytes 1048592 | tf_op jit(solution)/shard_map/all_gather | solution.py:48
  145.4 1.8 gather_fusion
  147.2 5.6 fusion.74
  152.8 3.3 fusion.43
  156.1 1.7 convolution_bitcast_fusion.1
  157.8 2.1 fusion.32
  159.9 5.4 fusion.76
  165.3 3.3 fusion.41
  168.7 2.1 fusion.34
  170.8 1.7 convolution_bitcast_fusion.3
  172.5 5.4 fusion.75
  177.9 3.2 fusion.42
  181.1 2.1 fusion.33
  183.3 1.7 convolution_bitcast_fusion.2
  185.0 5.4 fusion.77
  190.3 3.5 fusion.40
  195.8 3.5 fusion.5
  199.4 1.7 fusion.44
  203.4 1.7 fusion.46
  206.4 1.7 fusion.45
  210.9 3.5 fusion.17
  218.6 2.3 fusion.64
  220.9 2.4 fusion.63
  223.3 186.3 %all-reduce.4 = (bf16[64,8192]{1,0:T(8,128)(2,1)S(1)}, bf16[64,8192]{1,0:T(8,128)(2,1)}) all-reduce(f32[64,8192]{1,0:T(8,128)} %fusion.63, f32[64,8192]{1,0:T(8,128)S(1)} %fusion.64), channel_id=3, replica_groups=mesh['dp'=4,'seq'=32] {'seq'}, use_global_device_ids=true, to_apply=%region_13.0.clone | all-reduce | flops 1048576 | bytes 6291456
  410.7 8.6 convolution_bitcast_fusion
  419.3 21.3 %copy.209 = f32[5120,1024]{1,0:T(8,128)} copy(f32[5120,1024]{0,1:T(8,128)} %convolution_bitcast_fusion) | data formatting | bytes 41943040
  440.7 1.7 copy-done.6
  442.5 1.6 multiply_convert_fusion
  444.1 2.6 copy.133
  446.7 1.6 multiply_convert_fusion.2
  448.4 2.6 copy.131
  450.9 1.6 multiply_convert_fusion.1
  452.6 2.6 copy.132
  455.2 1.6 multiply_convert_fusion.3
  456.8 2.6 copy.130
  459.5 4.6 pad_maximum_fusion
  464.0 701.8 %reduce-scatter.4.cloned.1.call-done = f32[40,1024]{1,0:T(8,128)} async-done(((f32[5120,1024]{1,0:T(8,128)}), f32[40,1024]{1,0:T(8,128)}) %reduce-scatter.4.cloned.1.call-update) | async-done | bytes 163856
  (111 shorter events, 17.9 us)
Async XLA Ops:
  7.2 403.5 %copy-start = (bf16[1,2,16,5120]{3,2,1,0:T(8,128)(2,1)S(1)}, bf16[1,2,16,5120]{3,2,1,0:T(8,128)(2,1)}, u32[]{:S(2)}) copy-start(bf16[1,2,16,5120]{3,2,1,0:T(8,128)(2,1)} %param.11) | copy-start | bytes 983044
  7.2 71.8 %all-gather.5.cloned.1.call-start = ((), (), s32[]{:S(2)}) async-start(), calls=%async_computation.2 | async-start | bytes 1081344 | tf_op jit(solution)/shard_map/all_gather | solution.py:49
  7.9 137.4 %all-gather.3.cloned.1.call-start = ((), (), s32[]{:S(2)}) async-start(), calls=%async_computation.1 | async-start | bytes 1081344 | tf_op jit(solution)/shard_map/all_gather | solution.py:48
  8.7 1157.2 %reduce-scatter.4.cloned.1.call-start = ((), (), s32[]{:S(2)}) async-start(), calls=%async_computation.3 | async-start | bytes 21135360
  29.5 4.9 copy-start.37
  147.2 37.8 %copy-start.19 = (bf16[32,16,512]{2,1,0:T(8,128)(2,1)}, bf16[32,16,512]{2,1,0:T(8,128)(2,1)S(1)}, u32[]{:S(2)}) copy-start(bf16[32,16,512]{2,1,0:T(8,128)(2,1)S(1)} %gather_fusion) | copy-start | bytes 1572868
  152.8 3.3 copy-start.28
  152.8 3.4 copy-start.3
  165.3 3.3 copy-start.30
  165.3 3.4 copy-start.1
  177.9 3.3 copy-start.32
  190.3 3.5 copy-start.21
  194.5 1.3 copy-start.4
  194.5 1.3 copy-start.29
  194.5 1.3 copy-start.34
  194.5 6.6 slice-start
  195.8 3.6 copy-start.18
  195.8 5.3 slice-start.1
  195.8 5.3 copy-start.31
  195.8 5.3 copy-start.35
  199.4 3.2 copy-start.5
  199.4 2.3 copy-start.2
  199.4 5.6 slice-start.2
  201.7 1.7 copy-start.17
  201.7 3.3 slice-start.3
  203.4 2.6 copy-start.7
  203.4 1.7 copy-start.33
  203.4 1.7 copy-start.36
  205.0 1.3 copy-start.16
  206.4 1.7 copy-start.9
  206.4 1.7 copy-start.22
  206.4 1.7 copy-start.23
  206.4 1.7 copy-start.24
  210.9 5.0 copy-start.15
  214.4 1.5 copy-start.11
  215.9 1.0 copy-start.25
  215.9 1.0 copy-start.26
  215.9 1.1 copy-start.27
  440.7 1.7 copy-start.6
  440.7 1.8 copy-start.20
  444.1 2.6 copy-start.8
  448.4 2.6 copy-start.10
  452.6 2.6 copy-start.12
  456.8 2.6 copy-start.13
  456.8 2.6 copy-start.14
Sparse Core Ops, SparseCore 0:
  11.0 67.9 all-gather.4
  81.9 63.3 all-gather.2
  440.8 725.0 reduce-scatter.3
where the time goes:
time: 1170 us
  waiting for transfers between devices  810 us (69%)
  blocking collectives  186 us (16%)
  local copies, waits for them, and re-layouts  72.6 us (6%)
  matrix products  69.4 us (6%)
  other arithmetic  18.8 us (2%)
  between operations  14.8 us (1%)
    unnamed x4, waiting for transfers between devices  703 us
    unnamed x1, blocking collectives  186 us
    all_gather x1, waiting for transfers between devices, per_device(): lax.all_gather(keys_in, 'seq', axis=1, tiled=True)  63.8 us
    all_gather x1, waiting for transfers between devices, per_device(): lax.all_gather(input_values, 'seq', axis=1, tiled=True)  43.3 us
    unnamed x94, local copies, waits for them, and re-layouts  42.5 us
  transfers between devices with their start and end apart: 3, of which 3 were waited for; matrix products, arithmetic and copies ran while one was open for 4% of the time, Pallas kernels for 0%

commit v1 on v0

--- a/solution.py
+++ b/solution.py
@@ -45,7 +45,9 @@
 
 def per_device(siblings, queries, grad_out, keys_in, input_values, summary):
     keys_all, values_all = (
-        lax.all_gather(keys_in, "seq", axis=1, tiled=True),
+        jnp.concatenate(
+            lax.all_to_all(jnp.stack([keys_in] * lax.axis_size("seq")), "seq", 0, 0), axis=1
+        ),
         lax.all_gather(input_values, "seq", axis=1, tiled=True),
     )
     sibling = siblings[0]

time: 1170 us -> 1080 us (0.923)
  waiting for transfers between devices: 810 us -> 700 us
  local copies, waits for them, and re-layouts: 72.6 us -> 84.3 us
    all_gather x1 -> x0, waiting for transfers between devices: 63.8 us -> none  [per_device(): lax.all_gather(keys_in, 'seq', axis=1, tiled=True)]
    all_gather x1, waiting for transfers between devices: 43.3 us -> 0.01 us  [per_device(): lax.all_gather(input_values, 'seq', axis=1, tiled=True)]
    unnamed x94 -> x102, local copies, waits for them, and re-layouts: 42.5 us -> 46 us
    unnamed x4 -> x3, waiting for transfers between devices: 703 us -> 700 us
  transfers between devices with their start and end apart: 3 -> 3, of which waited for: 3 -> 1; matrix products, arithmetic and copies ran while one was open for 4% -> 9% of each run, Pallas kernels for 0% -> 0%
where the time goes in v1:
time: 1080 us
  waiting for transfers between devices  700 us (65%)
  blocking collectives  191 us (18%)
  local copies, waits for them, and re-layouts  84.3 us (8%)
  matrix products  66 us (6%)
  between operations  15.2 us (1%)
  other arithmetic  15.1 us (1%)
  starting transfers between devices  11.6 us (1%)
    unnamed x3, waiting for transfers between devices  700 us
    unnamed x1, blocking collectives  191 us
    unnamed x102, local copies, waits for them, and re-layouts  46 us
  transfers between devices with their start and end apart: 3, of which 1 were waited for; matrix products, arithmetic and copies ran while one was open for 9% of the time, Pallas kernels for 0%

profile of v1, /device:TPU:1, one launch (start us, length us, event | category | flops | bytes accessed | tf_op | source)
XLA Modules:
  0.0 1083.5 jit_solution(11455079794841888638)
XLA Ops:
  7.9 1.9 stack.2
  9.8 11.5 %all-to-all-start = ((bf16[32,1,2,16,512]{4,3,2,1,0:T(8,128)(2,1)}), bf16[32,1,2,16,512]{4,3,2,1,0:T(8,128)(2,1)}, u32[]{:S(2)}, u32[]{:S(2)}) async-start(bf16[32,1,2,16,512]{4,3,2,1,0:T(8,128)(2,1)} %stack.2), calls=%async_computation | async-start | bytes 2097152 | tf_op jit(solution)/shard_map/all_to_all | solution.py:49
  21.5 4.6 fusion.72
  26.1 2.4 copy.210
  28.5 2.4 copy.214
  30.9 1.5 copy.212
  32.4 1.5 copy.216
  33.9 4.6 fusion.73
  38.5 2.4 copy.211
  40.9 2.5 copy.215
  44.9 1.5 copy.217
  47.6 1.8 gather_fusion
  49.5 6.1 fusion.74
  55.6 4.1 fusion.76
  59.7 4.1 fusion.75
  63.7 3.4 fusion.43
  67.2 1.7 convolution_bitcast_fusion.1
  70.2 1.6 convolution_bitcast_fusion.3
  72.7 1.5 copy-done.3
  74.2 1.7 convolution_bitcast_fusion.2
  75.9 6.0 fusion.77
  81.9 3.3 fusion.40
  88.9 2.5 copy.142
  91.4 2.4 reshape.137
  93.8 3.9 fusion.63
  97.6 2.6 gather_fusion.1
  100.3 2.1 fusion.32
  102.8 1.6 fusion.34
  105.0 1.6 fusion.33
  107.2 1.6 fusion.35
  108.9 3.5 fusion.5
  123.3 2.5 copy.137
  125.8 2.4 reshape.135
  128.2 3.6 fusion.64
  131.8 190.8 %all-reduce.4 = (bf16[64,8192]{1,0:T(8,128)(2,1)}, bf16[64,8192]{1,0:T(8,128)(2,1)}) all-reduce(f32[64,8192]{1,0:T(8,128)} %fusion.63, f32[64,8192]{1,0:T(8,128)} %fusion.64), channel_id=3, replica_groups=mesh['dp'=4,'seq'=32] {'seq'}, use_global_device_ids=true, to_apply=%region_13.0.clone | all-reduce | flops 1048576 | bytes 6291456
  322.6 1.7 dynamic-slice_convert_fusion
  325.1 8.7 convolution_bitcast_fusion
  333.8 21.3 %copy.208 = f32[5120,1024]{1,0:T(8,128)} copy(f32[5120,1024]{0,1:T(8,128)} %convolution_bitcast_fusion) | data formatting | bytes 41943040
  355.1 1.7 multiply_convert_fusion
  356.8 2.6 copy.132
  359.4 1.7 multiply_convert_fusion.2
  361.1 2.6 copy.130
  363.7 1.6 multiply_convert_fusion.1
  365.3 2.6 copy.131
  368.0 1.6 multiply_convert_fusion.3
  369.6 2.6 copy.129
  372.2 4.6 pad_maximum_fusion
  376.8 699.8 %reduce-scatter.4.cloned.1.call-done = f32[40,1024]{1,0:T(8,128)} async-done(((f32[5120,1024]{1,0:T(8,128)}), f32[40,1024]{1,0:T(8,128)}) %reduce-scatter.4.cloned.1.call-update) | async-done | bytes 163856
  (121 shorter events, 21.7 us)
Async XLA Ops:
  7.2 317.9 %copy-start = (bf16[1,2,16,5120]{3,2,1,0:T(8,128)(2,1)S(1)}, bf16[1,2,16,5120]{3,2,1,0:T(8,128)(2,1)}, u32[]{:S(2)}) copy-start(bf16[1,2,16,5120]{3,2,1,0:T(8,128)(2,1)} %param.11) | copy-start | bytes 983044
  7.2 14.2 %copy-start.36 = (s32[1,2,16]{2,1,0:T(2,128)S(1)}, s32[1,2,16]{2,1,0:T(2,128)}, u32[]{:S(2)}) copy-start(s32[1,2,16]{2,1,0:T(2,128)} %param.6) | copy-start | bytes 388
  7.2 90.5 %all-gather.2.cloned.1.call-start = ((), (), s32[]{:S(2)}) async-start(), calls=%async_computation.2 | async-start | bytes 1081344 | tf_op jit(solution)/shard_map/all_gather | solution.py:51
  9.8 37.8 %all-to-all-start = ((bf16[32,1,2,16,512]{4,3,2,1,0:T(8,128)(2,1)}), bf16[32,1,2,16,512]{4,3,2,1,0:T(8,128)(2,1)}, u32[]{:S(2)}, u32[]{:S(2)}) async-start(bf16[32,1,2,16,512]{4,3,2,1,0:T(8,128)(2,1)} %stack.2), calls=%async_computation | async-start | bytes 2097152 | tf_op jit(solution)/shard_map/all_to_all | solution.py:49
  21.3 1055.3 %reduce-scatter.4.cloned.1.call-start = ((), (), s32[]{:S(2)}) async-start(), calls=%async_computation.3 | async-start | bytes 21135360
  43.4 3.0 copy-start.37
  49.5 6.1 copy-start.26
  55.6 4.1 copy-start.24
  63.7 3.4 copy-start.13
  63.7 5.1 copy-start.29
  67.2 4.7 slice-start
  68.9 1.3 copy-start.11
  68.9 3.0 slice-start.1
  69.7 3.0 copy-start.1
  71.9 2.3 copy-start.9
  72.7 1.5 copy-start.3
  81.9 4.9 copy-start.7
  85.2 1.5 copy-start.5
  85.2 2.5 copy-start.31
  85.3 2.5 copy-start.32
  85.3 2.5 copy-start.33
  100.3 2.2 copy-start.2
  100.3 2.6 copy-start.12
  102.8 1.8 copy-start.4
  102.8 2.2 copy-start.10
  105.0 1.8 copy-start.6
  105.0 2.2 copy-start.8
  105.0 3.8 copy-start.30
  105.0 3.8 copy-start.35
  107.2 1.7 copy-start.14
  107.2 6.2 slice-start.4
  108.8 3.6 copy-start.28
  108.9 4.6 slice-start.5
  112.4 3.6 slice-start.2
  113.4 1.6 copy-start.27
  113.4 2.6 slice-start.3
  115.0 1.9 copy-start.15
  115.0 4.3 slice-start.6
  116.0 2.3 copy-start.25
  116.0 3.3 slice-start.7
  118.4 1.9 copy-start.17
  119.4 1.3 copy-start.23
  120.7 1.6 copy-start.19
  356.8 2.6 copy-start.16
  361.1 2.6 copy-start.18
  365.3 2.6 copy-start.20
  369.6 2.6 copy-start.21
  369.6 2.6 copy-start.22
  (1 other events, 1.0 us)
Sparse Core Ops, SparseCore 0:
  11.0 71.9 all-gather.1
  355.2 721.3 reduce-scatter.3
